TPU v7x, 1024 devices: a whole 4x4x32 slice. The times are simulated.
1024 devices in a mesh: blk: 256 (over x_hi, y, z), mp: 4 (over x_lo, core).
Axes of the slice: x: 4 (x_hi: 2, x_lo: 2; x = x_hi * 2 + x_lo), y: 4, z: 32, core: 2. Of those that a mesh axis runs over, the one named last changes fastest.
Arguments:
- queries: bfloat16 [98304, 2560], P('blk', 'mp'), may hold values from -11 to 11
- keys: bfloat16 [32768, 2560], P('blk', 'mp'), may hold values from -11 to 11
- values: bfloat16 [32768, 2560], P('blk', 'mp'), may hold values from -6 to 6
- out_weight: bfloat16 [2560, 5120], P('mp'), may hold values from -0.125 to 0.125
Outputs:
- mixed: bfloat16 [98304, 5120], P('blk', 'mp')
All inputs are finite; a program needn't handle non-finite values.
Results may differ from a plain program's by a relative error of at most 0.018.
Values may be sent and summed in bfloat16 or wider, within the bound.
A program may use at most 32 MiB of HBM per device.

v0:
```python
import math

import jax
import jax.numpy as jnp
from jax import lax
from jax.sharding import PartitionSpec as P

HS = 128


def from_behind(value, axis, steps):
    count = lax.axis_size(axis)
    pairs = [(source, (source + steps) % count) for source in range(count)]
    return lax.ppermute(value, axis, pairs)


def fold_block(state, stacked_blocks, query_heads):
    running_max, running_sum, numerator = state
    head_count = query_heads.shape[1]
    key_heads = stacked_blocks[0].reshape(stacked_blocks.shape[1], head_count, HS)
    value_heads = stacked_blocks[1].reshape(stacked_blocks.shape[1], head_count, HS)
    scores = jnp.einsum("qhd,khd->qhk", query_heads, key_heads, preferred_element_type=jnp.float32)
    scores = scores * (1.0 / math.sqrt(HS))
    new_max = jnp.maximum(running_max, jnp.max(scores, axis=-1))
    rescale = jnp.exp(running_max - new_max)
    weights = jnp.exp(scores - new_max[:, :, None])
    new_sum = running_sum * rescale + jnp.sum(weights, axis=-1)
    product = jnp.einsum(
        "qhk,khd->qhd",
        weights.astype(jnp.bfloat16),
        value_heads,
        preferred_element_type=jnp.float32,
    )
    new_numerator = numerator * rescale[:, :, None] + product
    return (new_max, new_sum, new_numerator)


def on_device(queries, keys, values, out_weight):
    row_count = queries.shape[0]
    head_count = queries.shape[1] // HS
    query_heads = queries.reshape(row_count, head_count, HS)
    state = (
        jnp.full((row_count, head_count), -jnp.inf, jnp.float32),
        jnp.zeros((row_count, head_count), jnp.float32),
        jnp.zeros((row_count, head_count, HS), jnp.float32),
    )
    stacked_blocks = jnp.stack((keys, values))
    moving = from_behind(stacked_blocks, "blk", -2)
    state = fold_block(state, moving, query_heads)
    for repeat in range(4):
        moving = from_behind(moving, "blk", 1)
        state = fold_block(state, moving, query_heads)
    running_max, running_sum, numerator = state
    attended = (
        (numerator / running_sum[:, :, None])
        .reshape(row_count, head_count * HS)
        .astype(jnp.bfloat16)
    )
    window_partial_sum = jnp.dot(attended, out_weight, preferred_element_type=jnp.float32)
    summed = lax.psum_scatter(
        window_partial_sum.astype(jnp.bfloat16), "mp", scatter_dimension=1, tiled=True
    )
    return summed


def solution(mesh):
    placed = (P("blk", "mp"), P("blk", "mp"), P("blk", "mp"), P("mp", None))
    return jax.shard_map(
        on_device, mesh=mesh, in_specs=placed, out_specs=P("blk", "mp"), check_vma=False
    )
```

profile of v0, /device:TPU:1, one launch (start us, length us, event | category | flops | bytes accessed | tf_op | source)
XLA Modules:
  0.0 163.7 jit_solution(15904807745611875381)
XLA Ops:
  6.5 1.1 copy.20
  7.6 1.1 copy.21
  8.7 24.6 %collective-permute-start = (bf16[2,128,640]{1,2,0:T(8,128)(2,1)S(1)}, bf16[2,128,640]{1,2,0:T(8,128)(2,1)S(1)}, u32[]{:S(2)}, u32[]{:S(2)}) collective-permute-start(bf16[2,128,640]{1,2,0:T(8,128)(2,1)S(1)} %pad_maximum_fusion), channel_id=1, source_target_pairs={{0,1016},{4,1020},{8,0},{12,4},{16,8},{20,12},{24,16},{28,20},{32,... | collective-permute-start | bytes 983048 | tf_op jit(solution)/shard_map/ppermute | solution.py:14
  33.3 1.3 copy.22
  34.6 12.7 %collective-permute-done = bf16[2,128,640]{1,2,0:T(8,128)(2,1)S(1)} collective-permute-done((bf16[2,128,640]{1,2,0:T(8,128)(2,1)S(1)}, bf16[2,128,640]{1,2,0:T(8,128)(2,1)S(1)}, u32[]{:S(2)}, u32[]{:S(2)}) %collective-permute-start) | collective-permute-done | bytes 327712 | tf_op jit(solution)/shard_map/ppermute | solution.py:14
  47.3 1.9 %collective-permute-start.1 = (bf16[2,128,640]{1,2,0:T(8,128)(2,1)S(1)}, bf16[2,128,640]{1,2,0:T(8,128)(2,1)S(1)}, u32[]{:S(2)}, u32[]{:S(2)}) collective-permute-start(bf16[2,128,640]{1,2,0:T(8,128)(2,1)S(1)} %collective-permute-done), channel_id=1, source_target_pairs={{0,4},{4,8},{8,12},{12,16},{16,20},{20,24},{24,28},{28,32},{32,36}... | collective-permute-start | bytes 983048 | tf_op jit(solution)/shard_map/ppermute | solution.py:14
  49.2 0.3 fusion.45
  49.7 13.4 %collective-permute-done.1 = bf16[2,128,640]{1,2,0:T(8,128)(2,1)S(1)} collective-permute-done((bf16[2,128,640]{1,2,0:T(8,128)(2,1)S(1)}, bf16[2,128,640]{1,2,0:T(8,128)(2,1)S(1)}, u32[]{:S(2)}, u32[]{:S(2)}) %collective-permute-start.1) | collective-permute-done | bytes 327712 | tf_op jit(solution)/shard_map/ppermute | solution.py:14
  63.2 1.9 %collective-permute-start.2 = (bf16[2,128,640]{1,2,0:T(8,128)(2,1)S(1)}, bf16[2,128,640]{1,2,0:T(8,128)(2,1)S(1)}, u32[]{:S(2)}, u32[]{:S(2)}) collective-permute-start(bf16[2,128,640]{1,2,0:T(8,128)(2,1)S(1)} %collective-permute-done.1), channel_id=1, source_target_pairs={{0,4},{4,8},{8,12},{12,16},{16,20},{20,24},{24,28},{28,32},{32,36}... | collective-permute-start | bytes 983048 | tf_op jit(solution)/shard_map/ppermute | solution.py:14
  65.1 0.3 fusion.46
  65.5 12.6 %collective-permute-done.2 = bf16[2,128,640]{1,2,0:T(8,128)(2,1)S(1)} collective-permute-done((bf16[2,128,640]{1,2,0:T(8,128)(2,1)S(1)}, bf16[2,128,640]{1,2,0:T(8,128)(2,1)S(1)}, u32[]{:S(2)}, u32[]{:S(2)}) %collective-permute-start.2) | collective-permute-done | bytes 327712 | tf_op jit(solution)/shard_map/ppermute | solution.py:14
  78.1 1.9 %collective-permute-start.3 = (bf16[2,128,640]{1,2,0:T(8,128)(2,1)S(1)}, bf16[2,128,640]{1,2,0:T(8,128)(2,1)S(1)}, u32[]{:S(2)}, u32[]{:S(2)}) collective-permute-start(bf16[2,128,640]{1,2,0:T(8,128)(2,1)S(1)} %collective-permute-done.2), channel_id=1, source_target_pairs={{0,4},{4,8},{8,12},{12,16},{16,20},{20,24},{24,28},{28,32},{32,36}... | collective-permute-start | bytes 983048 | tf_op jit(solution)/shard_map/ppermute | solution.py:14
  80.1 0.3 fusion.44
  80.4 11.7 %collective-permute-done.3 = bf16[2,128,640]{1,2,0:T(8,128)(2,1)S(1)} collective-permute-done((bf16[2,128,640]{1,2,0:T(8,128)(2,1)S(1)}, bf16[2,128,640]{1,2,0:T(8,128)(2,1)S(1)}, u32[]{:S(2)}, u32[]{:S(2)}) %collective-permute-start.3) | collective-permute-done | bytes 327712 | tf_op jit(solution)/shard_map/ppermute | solution.py:14
  92.1 1.9 %collective-permute-start.4 = (bf16[2,128,640]{1,2,0:T(8,128)(2,1)S(1)}, bf16[2,128,640]{1,2,0:T(8,128)(2,1)S(1)}, u32[]{:S(2)}, u32[]{:S(2)}) collective-permute-start(bf16[2,128,640]{1,2,0:T(8,128)(2,1)S(1)} %collective-permute-done.3), channel_id=1, source_target_pairs={{0,4},{4,8},{8,12},{12,16},{16,20},{20,24},{24,28},{28,32},{32,36}... | collective-permute-start | bytes 983048 | tf_op jit(solution)/shard_map/ppermute | solution.py:14
  94.1 0.3 fusion.43
  94.4 11.2 %collective-permute-done.4 = bf16[2,128,640]{1,2,0:T(8,128)(2,1)S(1)} collective-permute-done((bf16[2,128,640]{1,2,0:T(8,128)(2,1)S(1)}, bf16[2,128,640]{1,2,0:T(8,128)(2,1)S(1)}, u32[]{:S(2)}, u32[]{:S(2)}) %collective-permute-start.4) | collective-permute-done | bytes 327712 | tf_op jit(solution)/shard_map/ppermute | solution.py:14
  105.7 0.3 fusion.42
  107.3 0.3 fusion.5
  107.6 0.3 fusion.3
  108.2 0.6 slice-done
  108.9 0.9 slice-done.1
  109.8 4.9 %convolution_convert_fusion = bf16[384,5120]{1,0:T(8,128)(2,1)} fusion(bf16[384,640]{0,1:T(8,128)(2,1)S(1)} %bitcast.80, bf16[640,5120]{1,0:T(8,128)(2,1)S(1)} %bitcast.79), kind=kOutput, calls=%fused_computation | convolution fusion | flops 2518548480 | bytes 10977280 | tf_op jit(solution)/shard_map/dot_general | solution.py:59
  114.7 42.2 %reduce-scatter.2.cloned.1.call-done = bf16[384,1280]{1,0:T(8,128)(2,1)} async-done(((bf16[384,5120]{1,0:T(8,128)(2,1)}), bf16[384,1280]{1,0:T(8,128)(2,1)}) %reduce-scatter.2.cloned.1.call-update) | async-done | bytes 983056 | tf_op jit(solution)/shard_map/reduce_scatter | solution.py:60
  (19 shorter events, 1.8 us)
Async XLA Ops:
  6.5 150.3 %reduce-scatter.2.cloned.1.call-start = ((), (), s32[]{:S(2)}) async-start(), calls=%async_computation.1 | async-start | bytes 4915200 | tf_op jit(solution)/shard_map/reduce_scatter | solution.py:60
  8.7 38.6 %collective-permute-start = (bf16[2,128,640]{1,2,0:T(8,128)(2,1)S(1)}, bf16[2,128,640]{1,2,0:T(8,128)(2,1)S(1)}, u32[]{:S(2)}, u32[]{:S(2)}) collective-permute-start(bf16[2,128,640]{1,2,0:T(8,128)(2,1)S(1)} %pad_maximum_fusion), channel_id=1, source_target_pairs={{0,1016},{4,1020},{8,0},{12,4},{16,8},{20,12},{24,16},{28,20},{32,... | collective-permute-start | bytes 983048 | tf_op jit(solution)/shard_map/ppermute | solution.py:14
  47.3 15.9 %collective-permute-start.1 = (bf16[2,128,640]{1,2,0:T(8,128)(2,1)S(1)}, bf16[2,128,640]{1,2,0:T(8,128)(2,1)S(1)}, u32[]{:S(2)}, u32[]{:S(2)}) collective-permute-start(bf16[2,128,640]{1,2,0:T(8,128)(2,1)S(1)} %collective-permute-done), channel_id=1, source_target_pairs={{0,4},{4,8},{8,12},{12,16},{16,20},{20,24},{24,28},{28,32},{32,36}... | collective-permute-start | bytes 983048 | tf_op jit(solution)/shard_map/ppermute | solution.py:14
  63.2 14.9 %collective-permute-start.2 = (bf16[2,128,640]{1,2,0:T(8,128)(2,1)S(1)}, bf16[2,128,640]{1,2,0:T(8,128)(2,1)S(1)}, u32[]{:S(2)}, u32[]{:S(2)}) collective-permute-start(bf16[2,128,640]{1,2,0:T(8,128)(2,1)S(1)} %collective-permute-done.1), channel_id=1, source_target_pairs={{0,4},{4,8},{8,12},{12,16},{16,20},{20,24},{24,28},{28,32},{32,36}... | collective-permute-start | bytes 983048 | tf_op jit(solution)/shard_map/ppermute | solution.py:14
  78.1 14.0 %collective-permute-start.3 = (bf16[2,128,640]{1,2,0:T(8,128)(2,1)S(1)}, bf16[2,128,640]{1,2,0:T(8,128)(2,1)S(1)}, u32[]{:S(2)}, u32[]{:S(2)}) collective-permute-start(bf16[2,128,640]{1,2,0:T(8,128)(2,1)S(1)} %collective-permute-done.2), channel_id=1, source_target_pairs={{0,4},{4,8},{8,12},{12,16},{16,20},{20,24},{24,28},{28,32},{32,36}... | collective-permute-start | bytes 983048 | tf_op jit(solution)/shard_map/ppermute | solution.py:14
  92.1 13.5 %collective-permute-start.4 = (bf16[2,128,640]{1,2,0:T(8,128)(2,1)S(1)}, bf16[2,128,640]{1,2,0:T(8,128)(2,1)S(1)}, u32[]{:S(2)}, u32[]{:S(2)}) collective-permute-start(bf16[2,128,640]{1,2,0:T(8,128)(2,1)S(1)} %collective-permute-done.3), channel_id=1, source_target_pairs={{0,4},{4,8},{8,12},{12,16},{16,20},{20,24},{24,28},{28,32},{32,36}... | collective-permute-start | bytes 983048 | tf_op jit(solution)/shard_map/ppermute | solution.py:14
  106.7 2.2 %slice-start = ((s8[6553600]{0:T(1024)(128)(4,1)}), s8[4194304]{0:T(1024)(128)(4,1)S(1)}, s32[]{:S(2)}) async-start(s8[6553600]{0:T(1024)(128)(4,1)} %bitcast.78), calls=%async_computation.2 | async-start | bytes 8388608
  107.3 2.5 %slice-start.1 = ((s8[6553600]{0:T(1024)(128)(4,1)}), s8[2359296]{0:T(1024)(128)(4,1)S(1)}, s32[]{:S(2)}) async-start(s8[6553600]{0:T(1024)(128)(4,1)} %bitcast.78), calls=%async_computation.3 | async-start | bytes 4718592
Sparse Core Ops, SparseCore 0:
  114.8 42.0 reduce-scatter.1
where the time goes:
time: 164 us
  waiting for transfers between devices  104 us (63%)
  starting transfers between devices  32.2 us (20%)
  between operations  13.6 us (8%)
  matrix products  8.02 us (5%)
  local copies, waits for them, and re-layouts  5.13 us (3%)
    ppermute x5, waiting for transfers between devices, from_behind(): return lax.ppermute(value, axis, pairs)  61.7 us
    reduce_scatter x1, waiting for transfers between devices, on_device(): lax.psum_scatter(window_partial_sum.astype(jnp.bfloat16), 'mp', scatter_d...  42.2 us
    ppermute x5, starting transfers between devices, from_behind(): return lax.ppermute(value, axis, pairs)  32.2 us
    unnamed x7, local copies, waits for them, and re-layouts  5.01 us
    dot_general x1, matrix products, on_device(): jnp.dot(attended, out_weight, preferred_element_type=jnp.float32)  4.85 us
  transfers between devices with their start and end apart: 6, of which 6 were waited for; matrix products, arithmetic and copies ran while one was open for 2% of the time, Pallas kernels for 0%

commit v1 on v0

v1 whole, which is shorter than its diff:
```python
import functools
import math

import jax
import jax.numpy as jnp
from jax import lax
from jax.experimental import pallas as pl
from jax.experimental.pallas import tpu as pltpu
from jax.sharding import PartitionSpec as P

HS = 128
MESH = pl.DeviceIdType.MESH
ROW_TILE = 128


def kernel(
    q_hbm, k_hbm, v_hbm, w_hbm, o_hbm,
    q, kv, w, att, acc, outgoing, incoming, result,
    kv_sem, load_sem, own_send, own_recv, on_send, on_recv,
    w_send, w_recv, att_send, att_recv, part_send, part_recv, out_sem,
):
    heads, _, window_rows, _ = kv.shape
    rows = q.shape[0]
    block = window_rows // 5
    pieces, _, width = outgoing.shape
    share = pieces * width

    blk, mp = lax.axis_index("blk"), lax.axis_index("mp")
    blocks = lax.axis_size("blk")
    ahead = {"blk": lax.rem(blk + 1, blocks)}
    behind = {"blk": lax.rem(blk + blocks - 1, blocks)}
    core = lax.rem(mp, 2)
    sibling = {"mp": mp + 1 - 2 * core}
    across = {"mp": lax.rem(mp + 2, 4)}

    def slot(j):
        return pl.ds(j * block, block)

    def columns_of(device):
        return pl.ds(pl.multiple_of(device * share, 128), share)

    kv_loads = []
    for h in range(heads):
        for side, ref in enumerate((k_hbm, v_hbm)):
            load = pltpu.make_async_copy(
                ref.at[:, pl.ds(h * HS, HS)], kv.at[h, side, slot(2)], kv_sem.at[h, side]
            )
            load.start()
            kv_loads.append(load)
    q_load = pltpu.make_async_copy(q_hbm, q, load_sem.at[0])
    q_load.start()

    for peer in (ahead, behind, sibling, across):
        pl.semaphore_signal(pltpu.get_barrier_semaphore(), inc=1, device_id=peer, device_id_type=MESH)
    pl.semaphore_wait(pltpu.get_barrier_semaphore(), 4)

    def kv_copy(h, source, target, peer, send, recv, way):
        return pltpu.make_async_remote_copy(
            src_ref=kv.at[h, :, slot(source)],
            dst_ref=kv.at[h, :, slot(target)],
            send_sem=send.at[way, h],
            recv_sem=recv.at[way, h],
            device_id=peer,
            device_id_type=MESH,
        )

    own_copies, on_copies = [], []
    for h in range(heads):
        kv_loads[2 * h].wait()
        kv_loads[2 * h + 1].wait()
        up = kv_copy(h, 2, 1, ahead, own_send, own_recv, 0)
        down = kv_copy(h, 2, 3, behind, own_send, own_recv, 1)
        up.start()
        down.start()
        own_copies.append((up, down))

    w_loads, w_copies = [], []
    for part, base in enumerate((lax.rem(mp + 2, 4), mp)):
        load = pltpu.make_async_copy(
            w_hbm.at[:, :, columns_of(base)],
            w.at[:, pl.ds(0, HS), pl.ds(part * share, share)],
            load_sem.at[1 + part],
        )
        load.start()
        w_loads.append(load)
        copy = pltpu.make_async_remote_copy(
            src_ref=w_hbm.at[:, :, columns_of(base + 1 - 2 * core)],
            dst_ref=w.at[:, pl.ds(HS, HS), pl.ds(part * share, share)],
            send_sem=w_send.at[part],
            recv_sem=w_recv.at[part],
            device_id=sibling,
            device_id_type=MESH,
        )
        copy.start()
        w_copies.append(copy)

    for h in range(heads):
        up = kv_copy(h, 1, 0, ahead, on_send, on_recv, 0)
        down = kv_copy(h, 3, 4, behind, on_send, on_recv, 1)
        own_copies[h][0].wait_recv()
        up.start()
        own_copies[h][1].wait_recv()
        down.start()
        on_copies.append((up, down))

    q_load.wait()
    scale = math.log2(math.e) / math.sqrt(HS)

    def attend(h):
        for r in range(0, rows, ROW_TILE):
            size = min(ROW_TILE, rows - r)
            query = q[pl.ds(r, size), pl.ds(h * HS, HS)]
            scores = lax.dot_general(
                query, kv[h, 0], (((1,), (1,)), ((), ())), preferred_element_type=jnp.float32
            )
            top = jnp.max(scores, axis=1, keepdims=True)
            weights = jnp.exp2(scores * scale - top * scale)
            total = jnp.sum(weights, axis=1, keepdims=True)
            numerator = jnp.dot(
                weights.astype(jnp.bfloat16), kv[h, 1], preferred_element_type=jnp.float32
            )
            att[h, pl.ds(r, size), pl.ds(0, HS)] = (numerator * (1.0 / total)).astype(jnp.bfloat16)

    def project(h, piece):
        return jnp.dot(
            att[h],
            w[h, :, pl.ds(pl.multiple_of(piece * width, 128), width)],
            preferred_element_type=jnp.float32,
        )

    def add_head(h):
        @pl.loop(0, 2 * pieces)
        def _(piece):
            if h == 0:
                acc[piece] = project(h, piece)
            else:
                acc[piece] += project(h, piece)

    att_copies = []
    for h in range(heads):
        on_copies[h][0].wait_recv()
        on_copies[h][1].wait_recv()
        attend(h)
        copy = pltpu.make_async_remote_copy(
            src_ref=att.at[h, :, pl.ds(0, HS)],
            dst_ref=att.at[h, :, pl.ds(HS, HS)],
            send_sem=att_send.at[h],
            recv_sem=att_recv.at[h],
            device_id=sibling,
            device_id_type=MESH,
        )
        copy.start()
        att_copies.append(copy)
        if h == 0:
            for load, arriving in zip(w_loads, w_copies):
                load.wait()
                arriving.wait_recv()
        else:
            att_copies[h - 1].wait_recv()
            add_head(h - 1)
    att_copies[heads - 1].wait_recv()

    def part_copy(piece):
        return pltpu.make_async_remote_copy(
            src_ref=outgoing.at[piece],
            dst_ref=incoming.at[piece],
            send_sem=part_send.at[piece],
            recv_sem=part_recv.at[piece],
            device_id=across,
            device_id_type=MESH,
        )

    for piece in range(pieces):
        outgoing[piece] = (acc[piece] + project(heads - 1, piece)).astype(jnp.bfloat16)
        part_copy(piece).start()

    @pl.loop(pieces, 2 * pieces)
    def _(piece):
        acc[piece] += project(heads - 1, piece)

    stores = []
    for piece in range(pieces):
        part_copy(piece).wait_recv()
        result[piece] = (acc[pieces + piece] + incoming[piece].astype(jnp.float32)).astype(jnp.bfloat16)
        store = pltpu.make_async_copy(
            result.at[piece], o_hbm.at[:, pl.ds(piece * width, width)], out_sem.at[piece]
        )
        store.start()
        stores.append(store)

    for up, down in own_copies + on_copies:
        up.wait_send()
        down.wait_send()
    for copy in w_copies + att_copies:
        copy.wait_send()
    for piece in range(pieces):
        part_copy(piece).wait_send()
    for store in stores:
        store.wait()


def on_device(queries, keys, values, out_weight):
    rows, features = queries.shape
    block = keys.shape[0]
    heads = features // HS
    share = out_weight.shape[1] // lax.axis_size("mp")
    pieces = 5 if share % (5 * 128) == 0 else 2
    width = share // pieces
    dma, bf16 = pltpu.SemaphoreType.DMA, jnp.bfloat16
    flops = 2 * rows * (2 * 5 * block * features + features * out_weight.shape[1])
    return pl.pallas_call(
        kernel,
        out_shape=jax.ShapeDtypeStruct((rows, share), bf16),
        in_specs=[pl.BlockSpec(memory_space=pltpu.HBM)] * 4,
        out_specs=pl.BlockSpec(memory_space=pl.ANY),
        scratch_shapes=[
            pltpu.VMEM((rows, features), bf16),
            pltpu.VMEM((heads, 2, 5 * block, HS), bf16),
            pltpu.VMEM((heads, 2 * HS, 2 * share), bf16),
            pltpu.VMEM((heads, rows, 2 * HS), bf16),
            pltpu.VMEM((2 * pieces, rows, width), jnp.float32),
            pltpu.VMEM((pieces, rows, width), bf16),
            pltpu.VMEM((pieces, rows, width), bf16),
            pltpu.VMEM((pieces, rows, width), bf16),
            dma((heads, 2)),
            dma((3,)),
            dma((2, heads)),
            dma((2, heads)),
            dma((2, heads)),
            dma((2, heads)),
            dma((2,)),
            dma((2,)),
            dma((heads,)),
            dma((heads,)),
            dma((pieces,)),
            dma((pieces,)),
            dma((pieces,)),
        ],
        compiler_params=pltpu.CompilerParams(
            collective_id=0, has_side_effects=True, vmem_limit_bytes=48 * 2**20
        ),
        cost_estimate=pl.CostEstimate(
            flops=flops, bytes_accessed=9_000_000, transcendentals=5 * block * rows * heads
        ),
    )(queries, keys, values, out_weight.reshape(heads, HS, out_weight.shape[1]))


def solution(mesh):
    placed = (P("blk", "mp"), P("blk", "mp"), P("blk", "mp"), P("mp", None))
    return jax.shard_map(
        on_device, mesh=mesh, in_specs=placed, out_specs=P("blk", "mp"), check_vma=False
    )
```

time: 164 us -> 76 us (0.46)
  waiting for transfers between devices: 104 us -> 0 us
  Pallas kernels: 0 us -> 71.6 us
  starting transfers between devices: 32.2 us -> 0 us
  between operations: 13.6 us -> 0.01 us
  matrix products: 8.02 us -> 0 us
    pallas_call x0 -> x1, Pallas kernels: none -> 71.6 us  [on_device(): pl.pallas_call(kernel, out_shape=jax.ShapeDtypeStruct((rows, share), bf16...]
    ppermute x5 -> x0, waiting for transfers between devices: 61.7 us -> none  [from_behind(): return lax.ppermute(value, axis, pairs)]
    reduce_scatter x1 -> x0, waiting for transfers between devices: 42.2 us -> none  [on_device(): lax.psum_scatter(window_partial_sum.astype(jnp.bfloat16), 'mp', scatter_d...]
    ppermute x5 -> x0, starting transfers between devices: 32.2 us -> none  [from_behind(): return lax.ppermute(value, axis, pairs)]
    dot_general x11 -> x0, matrix products: 8.02 us -> none  [the longest x1 4.85 us: on_device(): jnp.dot(attended, out_weight, preferred_element_type=jnp.float32)]
  transfers between devices with their start and end apart: 6 -> 0, of which waited for: 6 -> 0; matrix products, arithmetic and copies ran while one was open for 2% -> 0% of each run, Pallas kernels for 0% -> 0%
where the time goes in v1:
time: 76 us; the launch traced here: 75.4 us
  Pallas kernels  71.6 us (94%)
  local copies, waits for them, and re-layouts  3.81 us (5%)
    pallas_call x1, Pallas kernels, on_device(): pl.pallas_call(kernel, out_shape=jax.ShapeDtypeStruct((rows, share), bf16...  71.6 us
    unnamed x7, local copies, waits for them, and re-layouts  3.81 us

profile of v1, /device:TPU:1, one launch (start us, length us, event | category | flops | bytes accessed | tf_op | source)
XLA Modules:
  0.0 75.4 jit_solution(14292212339921104079)
XLA Ops:
  0.0 0.0 copy-start
  0.0 1.0 %copy-done = bf16[384,640]{1,0:T(8,128)(2,1)S(1)} copy-done((bf16[384,640]{1,0:T(8,128)(2,1)S(1)}, bf16[384,640]{1,0:T(8,128)(2,1)}, u32[]{:S(2)}) %copy-start) | copy-done | bytes 491544
  1.0 0.0 copy-start.1
  1.0 0.9 %copy-done.1 = bf16[128,640]{1,0:T(8,128)(2,1)S(1)} copy-done((bf16[128,640]{1,0:T(8,128)(2,1)S(1)}, bf16[128,640]{1,0:T(8,128)(2,1)}, u32[]{:S(2)}) %copy-start.1) | copy-done | bytes 163864
  1.9 0.0 copy-start.2
  1.9 0.9 %copy-done.2 = bf16[128,640]{1,0:T(8,128)(2,1)S(1)} copy-done((bf16[128,640]{1,0:T(8,128)(2,1)S(1)}, bf16[128,640]{1,0:T(8,128)(2,1)}, u32[]{:S(2)}) %copy-start.2) | copy-done | bytes 163864
  2.9 71.6 %shard_map.46 = bf16[384,1280]{1,0:T(8,128)(2,1)S(1)} custom-call(bf16[384,640]{1,0:T(8,128)(2,1)S(1)} %copy-done, bf16[128,640]{1,0:T(8,128)(2,1)S(1)} %copy-done.1, bf16[128,640]{1,0:T(8,128)(2,1)S(1)} %copy-done.2, bf16[5,128,5120]{2,1,0:T(8,128)(2,1)} %bitcast.1), custom_call_target="tpu_custom_call" | custom-call | flops 3145728000 | bytes 9000000 | tf_op jit(solution)/shard_map/pallas_call | solution.py:211
  74.4 0.9 %copy.6 = bf16[384,1280]{1,0:T(8,128)(2,1)} copy(bf16[384,1280]{1,0:T(8,128)(2,1)S(1)} %shard_map.46) | data formatting | bytes 1966080
Async XLA Ops:
  0.0 1.0 %copy-start = (bf16[384,640]{1,0:T(8,128)(2,1)S(1)}, bf16[384,640]{1,0:T(8,128)(2,1)}, u32[]{:S(2)}) copy-start(bf16[384,640]{1,0:T(8,128)(2,1)} %q_hbm.1) | copy-start | bytes 1474564
  1.0 0.9 %copy-start.1 = (bf16[128,640]{1,0:T(8,128)(2,1)S(1)}, bf16[128,640]{1,0:T(8,128)(2,1)}, u32[]{:S(2)}) copy-start(bf16[128,640]{1,0:T(8,128)(2,1)} %k_hbm.1) | copy-start | bytes 491524
  1.9 0.9 %copy-start.2 = (bf16[128,640]{1,0:T(8,128)(2,1)S(1)}, bf16[128,640]{1,0:T(8,128)(2,1)}, u32[]{:S(2)}) copy-start(bf16[128,640]{1,0:T(8,128)(2,1)} %v_hbm.1) | copy-start | bytes 491524

commit v2 on v1

v2 whole, which is shorter than its diff:
```python
import math

import jax
import jax.numpy as jnp
from jax import lax
from jax.experimental import pallas as pl
from jax.experimental.pallas import tpu as pltpu
from jax.sharding import PartitionSpec as P

HS = 128
MESH = pl.DeviceIdType.MESH
ROW_TILE = 128
PIECE = 256
X_HALVES = 2
Y_CHIPS = 4


def kernel(
    q_hbm, k_hbm, v_hbm, w_hbm, o_hbm,
    q, kv, w, att, acc, result,
    kv_sem, load_sem, own_send, own_recv, on_send, on_recv, sib_send, sib_recv,
    wx_send, wx_recv, wy_send, wy_recv, hand_send, hand_recv, att_send, att_recv, out_sem, ready,
):
    heads, _, window_rows, _ = kv.shape
    rows = q.shape[0]
    block = window_rows // 5
    share = acc.shape[1]
    half = share // 2
    piece_width = min(PIECE, share)
    pieces = share // piece_width

    blk, mp = lax.axis_index("blk"), lax.axis_index("mp")
    blocks = lax.axis_size("blk")
    z_chips = blocks // (X_HALVES * Y_CHIPS)
    x_hi, y, z = blk // (blocks // 2), lax.rem(blk // z_chips, Y_CHIPS), lax.rem(blk, z_chips)
    x_lo, core = mp // 2, lax.rem(mp, 2)
    parity = lax.rem(y, 2)

    def device(b, lo, c):
        return {"blk": b, "mp": 2 * lo + c}

    ahead_blk, behind_blk = lax.rem(blk + 1, blocks), lax.rem(blk + blocks - 1, blocks)
    other_blk = lax.rem(blk + blocks // 2, blocks)
    up_blk = blk + (lax.rem(y + 1, Y_CHIPS) - y) * z_chips
    down_blk = blk + (lax.rem(y + Y_CHIPS - 1, Y_CHIPS) - y) * z_chips
    ahead, behind = device(ahead_blk, x_lo, core), device(behind_blk, x_lo, core)
    y_up, y_down = device(up_blk, x_lo, core), device(down_blk, x_lo, core)
    sibling, across = device(blk, x_lo, 1 - core), device(blk, 1 - x_lo, core)

    def mover(b, lo):
        return device(b, lo, 1 - b // (blocks // 2))

    def greeter(b, lo):
        return device(b, lo, b // (blocks // 2))

    moves_weights = core != x_hi

    def slot(j):
        return pl.ds(j * block, block)

    def columns_of(lo, c):
        return pl.ds(pl.multiple_of((2 * lo + c) * share, 128), share)

    kv_loads = []
    for h in range(heads):
        for side, ref in enumerate((k_hbm, v_hbm)):
            load = pltpu.make_async_copy(
                ref.at[:, pl.ds(h * HS, HS)], kv.at[h, side, slot(2)], kv_sem.at[h, side]
            )
            load.start()
            kv_loads.append(load)

    barrier = pltpu.get_barrier_semaphore()

    def greet(*peers):
        for peer in peers:
            pl.semaphore_signal(barrier, inc=1, device_id=peer, device_id_type=MESH)

    greet(greeter(ahead_blk, x_lo), greeter(behind_blk, x_lo), across)

    @pl.when(moves_weights)
    def _():
        greet(mover(other_blk, 1 - x_lo), y_up, y_down, sibling)

    q_load = pltpu.make_async_copy(q_hbm, q, load_sem.at[0])
    q_load.start()
    w_load = pltpu.make_async_copy(
        w_hbm.at[:, :, :, columns_of(x_lo, core)], w.at[:, 0], load_sem.at[1]
    )
    w_load.start()

    pl.semaphore_wait(barrier, jnp.where(moves_weights, 4, 6))

    @pl.when(jnp.logical_not(moves_weights))
    def _():
        pl.semaphore_signal(ready, inc=1, device_id=sibling, device_id_type=MESH)

    def wx_copies(h):
        for chip in range(2):
            for own in range(2):
                target = 1 - core if chip == own else core
                yield pltpu.make_async_remote_copy(
                    src_ref=w_hbm.at[h, parity, :, columns_of(1 - x_lo, target)],
                    dst_ref=w.at[h, 2 + chip if own else 5 - chip, parity],
                    send_sem=wx_send.at[h, chip, own],
                    recv_sem=wx_recv.at[h, chip, own],
                    device_id=mover(other_blk if chip else blk, 1 - x_lo),
                    device_id_type=MESH,
                )

    def wy_copy(h, way):
        piece = (h, pl.ds(2, 4), parity, slice(None), pl.ds(way * half, half))
        return pltpu.make_async_remote_copy(
            src_ref=w.at[piece],
            dst_ref=w.at[piece],
            send_sem=wy_send.at[h, way],
            recv_sem=wy_recv.at[h, way],
            device_id=y_up if way else y_down,
            device_id_type=MESH,
        )

    def hand_over(h):
        return pltpu.make_async_remote_copy(
            src_ref=w.at[h, pl.ds(4, 2)],
            dst_ref=w.at[h, pl.ds(2, 2)],
            send_sem=hand_send.at[h],
            recv_sem=hand_recv.at[h],
            device_id=sibling,
            device_id_type=MESH,
        )

    def send_on_x(h):
        for copy in wx_copies(h):
            copy.start()

    def send_on_y(h):
        for copy in wx_copies(h):
            copy.wait_recv()
        wy_copy(h, 0).start()
        wy_copy(h, 1).start()
        for copy in wx_copies(h):
            copy.wait_send()
        if h + 2 < heads:
            send_on_x(h + 2)

    def move_when(condition, first, last):
        @pl.when(jnp.logical_and(moves_weights, condition))
        def _():
            for h in range(first, last):
                send_on_y(h)

    def give_weights(h):
        @pl.when(moves_weights)
        def _():
            wy_copy(h, 0).wait_recv()
            wy_copy(h, 1).wait_recv()
            hand_over(h).start()

    @pl.when(moves_weights)
    def _():
        for h in range(min(2, heads)):
            send_on_x(h)

    sib_copy = pltpu.make_async_remote_copy(
        src_ref=w_hbm.at[:, :, :, columns_of(x_lo, 1 - core)],
        dst_ref=w.at[:, 1],
        send_sem=sib_send,
        recv_sem=sib_recv,
        device_id=sibling,
        device_id_type=MESH,
    )

    early = min(3, heads)
    move_when(z == 0, 0, early)

    @pl.when(moves_weights)
    def _():
        pl.semaphore_wait(ready, 1)

    def kv_copy(h, source, target, peer, send, recv, way):
        return pltpu.make_async_remote_copy(
            src_ref=kv.at[h, :, slot(source)],
            dst_ref=kv.at[h, :, slot(target)],
            send_sem=send.at[way, h],
            recv_sem=recv.at[way, h],
            device_id=peer,
            device_id_type=MESH,
        )

    own_copies = [
        (
            kv_copy(h, 2, 1, ahead, own_send, own_recv, 0),
            kv_copy(h, 2, 3, behind, own_send, own_recv, 1),
        )
        for h in range(heads)
    ]
    on_copies = [
        (
            kv_copy(h, 1, 0, ahead, on_send, on_recv, 0),
            kv_copy(h, 3, 4, behind, on_send, on_recv, 1),
        )
        for h in range(heads)
    ]

    def send_own(h):
        kv_loads[2 * h].wait()
        kv_loads[2 * h + 1].wait()
        for copy in own_copies[h]:
            copy.start()

    def pass_block(h, way):
        own_copies[h][way].wait_recv()
        on_copies[h][way].start()

    for h in range(heads):
        send_own(h)
    sib_copy.start()

    @pl.when(z <= 1)
    def _():
        for h in range(heads):
            pass_block(h, 1)

    move_when(z == 1, 0, heads - 1)
    for h in range(heads):
        pass_block(h, 0)
        if h % 2 == 1 and early < heads:
            move_when(z == 0, early, early + 1)
            early += 1

    @pl.when(z > 1)
    def _():
        for h in range(heads):
            pass_block(h, 1)

    move_when(z == 0, early, heads)
    move_when(z == 1, heads - 1, heads)
    move_when(z == 2, 0, heads)

    q_load.wait()
    scale = math.log2(math.e) / math.sqrt(HS)

    def attend(h):
        for r in range(0, rows, ROW_TILE):
            size = min(ROW_TILE, rows - r)
            query = q[pl.ds(r, size), pl.ds(h * HS, HS)]
            scores = lax.dot_general(
                kv[h, 0], query, (((1,), (1,)), ((), ())), preferred_element_type=jnp.float32
            )
            top = jnp.max(scores, axis=0, keepdims=True)
            weights = jnp.exp2(scores * scale - top * scale)
            total = jnp.sum(weights, axis=0, keepdims=True)
            numerator = lax.dot_general(
                kv[h, 1],
                weights.astype(jnp.bfloat16),
                (((0,), (0,)), ((), ())),
                preferred_element_type=jnp.float32,
            )
            att[h, 0, pl.ds(r, size), :] = (numerator * (1.0 / total)).T.astype(jnp.bfloat16)

    def att_copy(h, source, target, peer):
        return pltpu.make_async_remote_copy(
            src_ref=att.at[h, source],
            dst_ref=att.at[h, target],
            send_sem=att_send.at[h, target - 1],
            recv_sem=att_recv.at[h, target - 1],
            device_id=peer,
            device_id_type=MESH,
        )

    def to_sibling(h):
        return att_copy(h, 0, 1, sibling)

    def to_across(h):
        return att_copy(h, 0, 2, across)

    def pass_on(h):
        return att_copy(h, 2, 3, sibling)

    def project(h, piece):
        columns = pl.ds(piece * piece_width, piece_width)
        gathered = jnp.concatenate([att[h, s] for s in range(4)], axis=1)
        return jnp.dot(
            gathered,
            w[h, pl.ds(0, 4), :, :, columns].reshape(4 * HS, piece_width),
            preferred_element_type=jnp.float32,
        )

    def await_head(h):
        to_sibling(h).wait_recv()
        pass_on(h).wait_recv()

        @pl.when(jnp.logical_not(moves_weights))
        def _():
            hand_over(h).wait_recv()

    def forward_head(h):
        to_across(h).wait_recv()
        pass_on(h).start()

    def add_head(h):
        await_head(h)
        for piece in range(pieces):
            columns = pl.ds(piece * piece_width, piece_width)
            if h == 0:
                acc[:, columns] = project(h, piece)
            else:
                acc[:, columns] += project(h, piece)

    for h in range(heads):
        move_when(z > 2, h, h + 1)
        on_copies[h][0].wait_recv()
        on_copies[h][1].wait_recv()
        attend(h)
        to_across(h).start()
        to_sibling(h).start()
        if h >= 1:
            forward_head(h - 1)
            give_weights(h - 1)
        if h == 1:
            w_load.wait()
            sib_copy.wait_recv()
        if h >= 2:
            add_head(h - 2)
    forward_head(heads - 1)
    give_weights(heads - 1)
    if heads > 1:
        add_head(heads - 2)
    await_head(heads - 1)
    stores = []
    for piece in range(pieces):
        columns = pl.ds(piece * piece_width, piece_width)
        result[:, columns] = (acc[:, columns] + project(heads - 1, piece)).astype(jnp.bfloat16)
        store = pltpu.make_async_copy(
            result.at[:, columns], o_hbm.at[:, columns], out_sem.at[piece]
        )
        store.start()
        stores.append(store)

    sib_copy.wait_send()
    for h in range(heads):
        for copy in own_copies[h] + on_copies[h]:
            copy.wait_send()
        to_sibling(h).wait_send()
        to_across(h).wait_send()
        pass_on(h).wait_send()

    @pl.when(moves_weights)
    def _():
        for h in range(heads):
            wy_copy(h, 0).wait_send()
            wy_copy(h, 1).wait_send()
            hand_over(h).wait_send()

    for store in stores:
        store.wait()


def on_device(queries, keys, values, out_weight):
    rows, features = queries.shape
    block = keys.shape[0]
    heads = features // HS
    width = out_weight.shape[1]
    share = width // lax.axis_size("mp")
    pieces = share // min(PIECE, share)
    dma, bf16 = pltpu.SemaphoreType.DMA, jnp.bfloat16
    flops = 2 * rows * (2 * 5 * block * features + features * width)
    return pl.pallas_call(
        kernel,
        out_shape=jax.ShapeDtypeStruct((rows, share), bf16),
        in_specs=[pl.BlockSpec(memory_space=pl.ANY)] * 4,
        out_specs=pl.BlockSpec(memory_space=pl.ANY),
        scratch_shapes=[
            pltpu.VMEM((rows, features), bf16),
            pltpu.VMEM((heads, 2, 5 * block, HS), bf16),
            pltpu.VMEM((heads, 6, 2, HS // 2, share), bf16),
            pltpu.VMEM((heads, 4, rows, HS), bf16),
            pltpu.VMEM((rows, share), jnp.float32),
            pltpu.VMEM((rows, share), bf16),
            dma((heads, 2)),
            dma((2,)),
            dma((2, heads)),
            dma((2, heads)),
            dma((2, heads)),
            dma((2, heads)),
            dma,
            dma,
            dma((heads, 2, 2)),
            dma((heads, 2, 2)),
            dma((heads, 2)),
            dma((heads, 2)),
            dma((heads,)),
            dma((heads,)),
            dma((heads, 3)),
            dma((heads, 3)),
            dma((pieces,)),
            pltpu.SemaphoreType.REGULAR,
        ],
        compiler_params=pltpu.CompilerParams(
            collective_id=0, has_side_effects=True, vmem_limit_bytes=63 * 2**20
        ),
        cost_estimate=pl.CostEstimate(
            flops=flops, bytes_accessed=9_000_000, transcendentals=5 * block * rows * heads
        ),
    )(queries, keys, values, out_weight.reshape(heads, 2, HS // 2, width))


def solution(mesh):
    placed = (P("blk", "mp"), P("blk", "mp"), P("blk", "mp"), P("mp", None))
    return jax.shard_map(
        on_device, mesh=mesh, in_specs=placed, out_specs=P("blk", "mp"), check_vma=False
    )
```

time: 76 us -> 60.7 us (0.80)
  the two profiles are of different devices: /device:TPU:1 before, /device:TPU:29 now
where the time goes in v2:
time: 60.7 us; the launch traced here: 60.5 us
  Pallas kernels  58.3 us (96%)
  local copies, waits for them, and re-layouts  2.21 us (4%)
    pallas_call x1, Pallas kernels, on_device(): pl.pallas_call(kernel, out_shape=jax.ShapeDtypeStruct((rows, share), bf16...  58.3 us
    unnamed x1, local copies, waits for them, and re-layouts  2.21 us

profile of v2, /device:TPU:29, one launch (start us, length us, event | category | flops | bytes accessed | tf_op | source)
XLA Modules:
  0.0 60.5 jit_solution(12406956807359850018)
XLA Ops:
  0.0 58.3 %shard_map.46 = bf16[384,1280]{1,0:T(8,128)(2,1)} custom-call(bf16[384,640]{1,0:T(8,128)(2,1)} %q_hbm.1, bf16[128,640]{1,0:T(8,128)(2,1)} %k_hbm.1, bf16[128,640]{1,0:T(8,128)(2,1)} %v_hbm.1, bf16[5,2,64,5120]{3,2,1,0:T(8,128)(2,1)} %bitcast.1), custom_call_target="tpu_custom_call" | custom-call | flops 3145728000 | bytes 9000000 | tf_op jit(solution)/shard_map/pallas_call | solution.py:368
  58.3 2.2 %copy.6 = bf16[384,1280]{1,0:T(8,128)(2,1)} copy(bf16[384,1280]{1,0:T(8,128)(2,1)} %shard_map.46) | data formatting | bytes 1966080

commit v3 on v2

--- a/solution.py
+++ b/solution.py
@@ -171,6 +171,7 @@
     )
 
     early = min(3, heads)
+    late = jnp.logical_and(z >= max(z_chips - 2, 3), y > 0)
     move_when(z == 0, 0, early)
 
     @pl.when(moves_weights)
@@ -228,6 +229,8 @@
             move_when(z == 0, early, early + 1)
             early += 1
 
+    move_when(late, 0, 2)
+
     @pl.when(z > 1)
     def _():
         for h in range(heads):
@@ -236,6 +239,7 @@
     move_when(z == 0, early, heads)
     move_when(z == 1, heads - 1, heads)
     move_when(z == 2, 0, heads)
+    move_when(late, 2, heads)
 
     q_load.wait()
     scale = math.log2(math.e) / math.sqrt(HS)
@@ -308,24 +312,25 @@
                 acc[:, columns] += project(h, piece)
 
     for h in range(heads):
-        move_when(z > 2, h, h + 1)
+        move_when(jnp.logical_and(z > 2, jnp.logical_not(late)), h, h + 1)
         on_copies[h][0].wait_recv()
         on_copies[h][1].wait_recv()
         attend(h)
         to_across(h).start()
         to_sibling(h).start()
-        if h >= 1:
-            forward_head(h - 1)
-            give_weights(h - 1)
-        if h == 1:
+        if h == min(2, heads - 1):
             w_load.wait()
             sib_copy.wait_recv()
         if h >= 2:
-            add_head(h - 2)
-    forward_head(heads - 1)
-    give_weights(heads - 1)
-    if heads > 1:
-        add_head(heads - 2)
+            forward_head(h - 2)
+            give_weights(h - 2)
+        if h >= 3:
+            add_head(h - 3)
+    for h in range(max(heads - 2, 0), heads):
+        forward_head(h)
+        give_weights(h)
+        if h >= 1:
+            add_head(h - 1)
     await_head(heads - 1)
     stores = []
     for piece in range(pieces):

time: 60.7 us -> 58.8 us (0.969)
  the two profiles are of different devices: /device:TPU:29 before, /device:TPU:1005 now
where the time goes in v3:
time: 58.8 us; the launch traced here: 58.7 us
  Pallas kernels  56.4 us (96%)
  local copies, waits for them, and re-layouts  2.21 us (4%)
    pallas_call x1, Pallas kernels, on_device(): pl.pallas_call(kernel, out_shape=jax.ShapeDtypeStruct((rows, share), bf16...  56.4 us
    unnamed x1, local copies, waits for them, and re-layouts  2.21 us

profile of v3, /device:TPU:1005, one launch (start us, length us, event | category | flops | bytes accessed | tf_op | source)
XLA Modules:
  0.0 58.7 jit_solution(15510673154756929463)
XLA Ops:
  0.0 56.4 %shard_map.46 = bf16[384,1280]{1,0:T(8,128)(2,1)} custom-call(bf16[384,640]{1,0:T(8,128)(2,1)} %q_hbm.1, bf16[128,640]{1,0:T(8,128)(2,1)} %k_hbm.1, bf16[128,640]{1,0:T(8,128)(2,1)} %v_hbm.1, bf16[5,2,64,5120]{3,2,1,0:T(8,128)(2,1)} %bitcast.1), custom_call_target="tpu_custom_call" | custom-call | flops 3145728000 | bytes 9000000 | tf_op jit(solution)/shard_map/pallas_call | solution.py:373
  56.5 2.2 %copy.6 = bf16[384,1280]{1,0:T(8,128)(2,1)} copy(bf16[384,1280]{1,0:T(8,128)(2,1)} %shard_map.46) | data formatting | bytes 1966080
